TPU v7x, 32 devices: a whole 2x2x4 slice. The times are simulated.
32 devices in a mesh: mem: 8 (over z, core), tensor: 4 (over y, x).
Axes of the slice: x: 2, y: 2, z: 4, core: 2. Of those that a mesh axis runs over, the one named last changes fastest.
Arguments:
- tokens: bfloat16 [4096, 4096], P('mem', 'tensor'), may hold values from -6 to 6
- neighbours: int32 [64, 2, 2], replicated, may hold values from 0 to 63, as said below
- memory_bank: bfloat16 [512, 128, 896], P('mem', 'tensor'), may hold values from -340 to 340
- w_query: bfloat16 [4096, 4096], P(None, 'tensor'), may hold values from -0.09375 to 0.09375
- w_key: bfloat16 [896, 4096], P(None, 'tensor'), may hold values from -0.1875 to 0.1875
- w_value: bfloat16 [896, 4096], P(None, 'tensor'), may hold values from -0.1875 to 0.1875
- w_out: bfloat16 [4096, 4096], P('tensor', 'mem'), may hold values from -0.09375 to 0.09375
Outputs:
- mixed: bfloat16 [4096, 4096], P('mem', 'tensor')
Inputs may be any that keep to these rules, and one draw needn't show every extreme that they name: `neighbours`: among the 16 entries of the spans c with c // 8 equal to one value, no memory shard is named more than 2 times; some shard is named exactly 2 times for every such value.
All inputs are finite; a program needn't handle non-finite values.
Results may differ from a plain program's by a relative error of at most 0.014.
The roundings to bfloat16 on the way count: a program that leaves them out, or rounds other values in their place, can miss the bound.
Values may be sent and summed in bfloat16 or wider, within the bound.
A program may use at most 64 MiB of HBM per device.

v0:
```python
import math

import jax
import jax.numpy as jnp
from jax import lax
from jax.sharding import PartitionSpec as P

DH = 128
NB = 2


def body(tokens, neighbours, memory_bank, w_query, w_key, w_value, w_out):
    mem_count = lax.axis_size("mem")
    mem_index = lax.axis_index("mem")
    slice_len = memory_bank.shape[1]
    enc_width = memory_bank.shape[2]
    head_cols = w_query.shape[1]
    heads_here = head_cols // DH
    requests = neighbours.shape[0] * neighbours.shape[1] // mem_count
    spans_here = requests // NB
    slot_count = max(2, (requests + mem_count - 1) // mem_count)
    score_scale = 1.0 / math.sqrt(DH)
    query_sum = jnp.dot(
        lax.all_gather(tokens, "tensor", axis=1, tiled=True),
        w_query,
        preferred_element_type=jnp.float32,
    )
    queries = (query_sum * score_scale).astype(jnp.bfloat16)
    listing = neighbours.reshape(mem_count, requests, 2)
    owner_ids = listing[:, :, 0]
    row_ids = listing[:, :, 1]
    owned_here = owner_ids == mem_index
    slot_rank = jnp.cumsum(owned_here.astype(jnp.int32), axis=1) - 1
    slot_ids = jnp.arange(slot_count, dtype=jnp.int32)
    chosen = owned_here[:, None, :] & (slot_rank[:, None, :] == slot_ids[None, :, None])
    wanted = jnp.sum(jnp.where(chosen, row_ids[:, None, :], 0), axis=2)
    outgoing = jnp.take(memory_bank, wanted.reshape(-1), axis=0).reshape(
        mem_count, slot_count, slice_len, enc_width
    )
    incoming = lax.all_to_all(outgoing, "mem", split_axis=0, concat_axis=0, tiled=True)
    own_list = lax.dynamic_index_in_dim(listing, mem_index, 0, keepdims=False)
    own_owner = own_list[:, 0]
    positions = jnp.arange(requests, dtype=jnp.int32)
    earlier = positions[None, :] < positions[:, None]
    same_owner = own_owner[:, None] == own_owner[None, :]
    own_rank = jnp.sum((same_owner & earlier).astype(jnp.int32), axis=1)
    source = own_owner * slot_count + own_rank
    fetched = jnp.take(
        incoming.reshape(mem_count * slot_count, slice_len, enc_width), source, axis=0
    )
    joined = jnp.concatenate([w_key, w_value], axis=1)
    key_value = jnp.dot(
        lax.all_gather(fetched, "tensor", axis=1, tiled=True),
        joined,
        preferred_element_type=jnp.float32,
    ).astype(jnp.bfloat16)
    bank_len = key_value.shape[1]
    key_block = key_value[:, :, :head_cols].reshape(spans_here, NB * bank_len, heads_here, DH)
    value_block = key_value[:, :, head_cols:].reshape(spans_here, NB * bank_len, heads_here, DH)
    query_block = queries.reshape(spans_here, -1, heads_here, DH)
    scores = jnp.einsum(
        "cqhd,ckhd->chqk", query_block, key_block, preferred_element_type=jnp.float32
    )
    row_max = jnp.max(scores, axis=-1, keepdims=True)
    lifted = jnp.exp(scores - row_max)
    normed = lifted / jnp.sum(lifted, axis=-1, keepdims=True)
    weights = normed.astype(jnp.bfloat16)
    attended = jnp.einsum(
        "chqk,ckhd->cqhd", weights, value_block, preferred_element_type=jnp.float32
    )
    attended = attended.astype(jnp.bfloat16).reshape(-1, head_cols)
    partial_value = jnp.dot(
        attended,
        lax.all_gather(w_out, "mem", axis=1, tiled=True),
        preferred_element_type=jnp.float32,
    )
    summed = lax.psum_scatter(
        partial_value.astype(jnp.bfloat16), "tensor", scatter_dimension=1, tiled=True
    )
    return summed


def solution(mesh):
    return jax.shard_map(
        body,
        mesh=mesh,
        in_specs=(
            P("mem", "tensor"),
            P(),
            P("mem", "tensor", None),
            P(None, "tensor"),
            P(None, "tensor"),
            P(None, "tensor"),
            P("tensor", "mem"),
        ),
        out_specs=P("mem", "tensor"),
        check_vma=False,
    )
```

profile of v0, /device:TPU:0, one launch (start us, length us, event | category | flops | bytes accessed | tf_op | source)
XLA Modules:
  0.0 265.8 jit_solution(5257089275965303308)
XLA Ops:
  6.5 0.0 all-gather.6.cloned.1.call-start
  6.5 0.7 all-gather.6.cloned.1.call-update
  7.3 0.8 copy.17
  8.0 0.1 reshape.87
  8.1 0.2 reduce_window_sum.11
  8.3 0.1 select_reduce_fusion
  8.5 0.1 copy.19
  8.5 0.1 reshape.88
  8.6 0.1 copy.18
  8.8 2.7 %gather_fusion = bf16[16,32,896]{2,1,0:T(8,128)(2,1)S(1)} fusion(bf16[64,32,896]{2,1,0:T(8,128)(2,1)} %param.9, s32[1024]{0:T(1024)S(1)} %pad_clamp_fusion.1), kind=kCustom, calls=%fused_computation | custom fusion | bytes 1835072 | tf_op jit(solution)/shard_map/jit(_take)/gather | solution.py:37
  11.5 1.1 broadcast_select_fusion.1
  12.6 6.3 %all-to-all-start = ((bf16[8,2,32,896]{3,2,1,0:T(8,128)(2,1)}), bf16[8,2,32,896]{3,2,1,0:T(8,128)(2,1)S(1)}, u32[]{:S(2)}, u32[]{:S(2)}) async-start(bf16[8,2,32,896]{3,2,1,0:T(8,128)(2,1)} %broadcast_select_fusion.1), calls=%async_computation | async-start | bytes 1835008 | tf_op jit(solution)/shard_map/all_to_all | solution.py:40
  18.9 0.0 all-gather.4.cloned.1.call-start
  19.0 0.2 convert_reduce_fusion
  19.2 23.5 %all-to-all-done = bf16[8,2,32,896]{3,2,1,0:T(8,128)(2,1)S(1)} async-done(((bf16[8,2,32,896]{3,2,1,0:T(8,128)(2,1)}), bf16[8,2,32,896]{3,2,1,0:T(8,128)(2,1)S(1)}, u32[]{:S(2)}, u32[]{:S(2)}) %all-to-all-start) | async-done | bytes 917536 | tf_op jit(solution)/shard_map/all_to_all | solution.py:40
  42.7 0.7 gather_fusion.1
  43.4 1.1 broadcast_select_fusion
  44.5 0.0 all-gather.4.cloned.1.call-update
  44.5 0.0 all-gather.8.cloned.1.call-start
  44.6 0.7 all-gather.8.cloned.1.call-update
  45.3 0.0 copy-start.1
  45.3 0.0 reduce-scatter.2.cloned.1.call-start
  45.3 19.3 %all-gather.6.cloned.1.call-done = bf16[512,4096]{1,0:T(8,128)(2,1)} async-done(((bf16[512,1024]{1,0:T(8,128)(2,1)}), bf16[512,4096]{1,0:T(8,128)(2,1)}) %all-gather.6.cloned.1.call-update) | async-done | bytes 4194320 | tf_op jit(solution)/shard_map/all_gather | solution.py:24
  64.6 9.1 %fusion.14 = bf16[64,8,8,128]{3,1,2,0:T(8,128)(2,1)S(1)} fusion(bf16[512,4096]{1,0:T(8,128)(2,1)} %all-gather.6.cloned.1.call-done, bf16[4096,1024]{1,0:T(8,128)(2,1)} %param.10), kind=kOutput, calls=%fused_computation.18 | convolution fusion | flops 4296015872 | bytes 13631488 | tf_op jit(solution)/shard_map/dot_general | solution.py:23
  73.8 0.3 copy.24
  74.1 40.8 %all-gather.4.cloned.1.call-done = bf16[16,128,896]{2,1,0:T(8,128)(2,1)} async-done(((bf16[16,32,896]{2,1,0:T(8,128)(2,1)}), bf16[16,128,896]{2,1,0:T(8,128)(2,1)}) %all-gather.4.cloned.1.call-update) | async-done | bytes 3670032 | tf_op jit(solution)/shard_map/all_gather | solution.py:53
  114.9 0.0 copy-done.1
  114.9 11.1 %convolution_convert_fusion.1 = bf16[16,128,2048]{2,1,0:T(8,128)(2,1)S(1)} fusion(bf16[16,128,896]{2,1,0:T(8,128)(2,1)} %all-gather.4.cloned.1.call-done, bf16[896,1024]{1,0:T(8,128)(2,1)S(1)} %copy-done.1, bf16[896,1024]{1,0:T(8,128)(2,1)} %param.11), kind=kOutput, calls=%fused_computation.4 | convolution fusion | flops 7527727104 | bytes 15728640 | tf_op jit(solution)/shard_map/dot_general | solution.py:52
  126.0 1.5 fusion.26
  127.5 1.1 copy.25
  128.6 3.1 %copy.26 = bf16[256,8,8,128]{3,2,1,0:T(8,128)(2,1)} copy(bf16[256,8,8,128]{3,1,2,0:T(8,128)(2,1)S(1)} %bitcast.51) | data formatting | bytes 8388608
  131.6 1.6 fusion.3
  133.2 0.0 copy-start
  133.2 2.0 copy-done
  135.2 1.2 fusion.27
  136.3 12.0 %fusion.11 = bf16[8,64,8,128]{3,1,2,0:T(8,128)(2,1)S(1)} fusion(bf16[8,256,8,128]{3,2,1,0:T(8,128)(2,1)} %bitcast.54, f32[8,8,64]{2,1,0:T(8,128)S(1)} %fusion.27, f32[8,8,64,256]{3,2,1,0:T(8,128)} %copy-done), kind=kOutput, calls=%fused_computation.17 | convolution fusion | flops 272109824 | bytes 9453568 | tf_op jit(solution)/shard_map/chqk,ckhd->cqhd/dot_general | solution.py:68
  148.3 0.7 copy.23
  149.0 49.5 %all-gather.8.cloned.1.call-done = bf16[1024,4096]{1,0:T(8,128)(2,1)} async-done(((bf16[1024,512]{1,0:T(8,128)(2,1)}), bf16[1024,4096]{1,0:T(8,128)(2,1)}) %all-gather.8.cloned.1.call-update) | async-done | bytes 8388624 | tf_op jit(solution)/shard_map/all_gather | solution.py:74
  198.6 9.4 %convolution_convert_fusion = bf16[512,4096]{1,0:T(8,128)(2,1)} fusion(bf16[1024,4096]{1,0:T(8,128)(2,1)} %all-gather.8.cloned.1.call-done, bf16[64,8,8,128]{3,2,1,0:T(8,128)(2,1)S(1)} %bitcast.57), kind=kOutput, calls=%fused_computation.3 | convolution fusion | flops 4297064448 | bytes 13631488 | tf_op jit(solution)/shard_map/dot_general | solution.py:72
  207.9 0.0 reduce-scatter.2.cloned.1.call-update
  208.0 51.4 %reduce-scatter.2.cloned.1.call-done = bf16[512,1024]{1,0:T(8,128)(2,1)} async-done(((bf16[512,4096]{1,0:T(8,128)(2,1)}), bf16[512,1024]{1,0:T(8,128)(2,1)}) %reduce-scatter.2.cloned.1.call-update) | async-done | bytes 1048592 | tf_op jit(solution)/shard_map/reduce_scatter | solution.py:77
  (10 shorter events, 0.1 us)
Async XLA Ops:
  6.5 58.1 %all-gather.6.cloned.1.call-start = ((), (), s32[]{:S(2)}) async-start(), calls=%async_computation.3 | async-start | bytes 5242880 | tf_op jit(solution)/shard_map/all_gather | solution.py:24
  12.6 30.1 %all-to-all-start = ((bf16[8,2,32,896]{3,2,1,0:T(8,128)(2,1)}), bf16[8,2,32,896]{3,2,1,0:T(8,128)(2,1)S(1)}, u32[]{:S(2)}, u32[]{:S(2)}) async-start(bf16[8,2,32,896]{3,2,1,0:T(8,128)(2,1)} %broadcast_select_fusion.1), calls=%async_computation | async-start | bytes 1835008 | tf_op jit(solution)/shard_map/all_to_all | solution.py:40
  18.9 95.9 %all-gather.4.cloned.1.call-start = ((), (), s32[]{:S(2)}) async-start(), calls=%async_computation.2 | async-start | bytes 4587520 | tf_op jit(solution)/shard_map/all_gather | solution.py:53
  44.5 154.0 %all-gather.8.cloned.1.call-start = ((), (), s32[]{:S(2)}) async-start(), calls=%async_computation.4 | async-start | bytes 9437184 | tf_op jit(solution)/shard_map/all_gather | solution.py:74
  45.3 69.6 %copy-start.1 = (bf16[896,1024]{1,0:T(8,128)(2,1)S(1)}, bf16[896,1024]{1,0:T(8,128)(2,1)}, u32[]{:S(2)}) copy-start(bf16[896,1024]{1,0:T(8,128)(2,1)} %param.12) | copy-start | bytes 5505028
  45.3 214.0 %reduce-scatter.2.cloned.1.call-start = ((), (), s32[]{:S(2)}) async-start(), calls=%async_computation.5 | async-start | bytes 5242880 | tf_op jit(solution)/shard_map/reduce_scatter | solution.py:77
  133.2 2.0 copy-start
Sparse Core Ops, SparseCore 0:
  9.2 55.3 all-gather.5
  66.5 48.3 all-gather.3
  116.5 82.0 all-gather.7
  208.1 51.1 reduce-scatter.1
where the time goes:
time: 266 us
  waiting for transfers between devices  186 us (70%)
  matrix products  43.2 us (16%)
  between operations  13.3 us (5%)
  local copies, waits for them, and re-layouts  13.1 us (5%)
  starting transfers between devices  6.44 us (2%)
  other arithmetic  3.89 us (1%)
    reduce_scatter x1, waiting for transfers between devices, body(): lax.psum_scatter(partial_value.astype(jnp.bfloat16), 'tensor', scatter_di...  51.4 us
    all_gather x1, waiting for transfers between devices, body(): lax.all_gather(w_out, 'mem', axis=1, tiled=True)  49.5 us
    all_gather x1, waiting for transfers between devices, body(): lax.all_gather(fetched, 'tensor', axis=1, tiled=True)  40.8 us
    all_to_all x1, waiting for transfers between devices, body(): lax.all_to_all(outgoing, 'mem', split_axis=0, concat_axis=0, tiled=True)  23.5 us
    all_gather x1, waiting for transfers between devices, body(): lax.all_gather(tokens, 'tensor', axis=1, tiled=True)  19.3 us
    dot_general x1, matrix products, body(): jnp.einsum('chqk,ckhd->cqhd', weights, value_block, preferred_element_typ...  12 us
    dot_general x1, matrix products, body(): jnp.dot(lax.all_gather(fetched, 'tensor', axis=1, tiled=True), joined, pr...  11.1 us
    dot_general x1, matrix products, body(): jnp.dot(attended, lax.all_gather(w_out, 'mem', axis=1, tiled=True), prefe...  9.37 us
  transfers between devices with their start and end apart: 5, of which 5 were waited for; matrix products, arithmetic and copies ran while one was open for 18% of the time, Pallas kernels for 0%

commit v1 on v0

--- a/solution.py
+++ b/solution.py
@@ -1,8 +1,11 @@
+import functools
 import math
 
 import jax
 import jax.numpy as jnp
 from jax import lax
+from jax.experimental import pallas as pl
+from jax.experimental.pallas import tpu as pltpu
 from jax.sharding import PartitionSpec as P
 
 DH = 128
@@ -80,19 +83,390 @@
     return summed
 
 
+MESH = pl.DeviceIdType.MESH
+
+
+def fused_kernel(
+    mem_count, tensor_count, spans, score_scale,
+    source, tokens, outgoing, w_query, w_key, w_value, w_out, result,
+    tok, wq, wk, wv, enc, keys, values, acc, queries, attended, wo,
+    part_d, part_x, part_y, relay_x, relay_y, got_x, got_y,
+    load_sem, tok_send, tok_recv, bank_send, bank_recv, near_send, near_recv,
+    wo_send, wo_recv, core_send, core_recv, red_send, red_recv,
+):
+    me = lax.axis_index("mem")
+    t = lax.axis_index("tensor")
+    tx = t + 1 - 2 * (t % 2)
+    ty = (t + 2) % 4
+    td = (tx + 2) % 4
+    z_count = mem_count // 2
+    z = me // 2
+    core = me % 2
+    mate = me + 1 - 2 * core
+    rows = tok.shape[1]
+    half = rows // 2
+    width = tok.shape[2]
+    tile = 256
+
+    def remote(src, dst, send, recv, **where):
+        return pltpu.make_async_remote_copy(
+            src_ref=src, dst_ref=dst, send_sem=send, recv_sem=recv,
+            device_id=where, device_id_type=MESH,
+        )
+
+    def arrived(ref, send, recv):
+        remote(ref, ref, send, recv, tensor=tx).wait_recv()
+
+    def left(ref, send, recv):
+        remote(ref, ref, send, recv, tensor=tx).wait_send()
+
+    barrier = pltpu.get_barrier_semaphore()
+    for d in range(1, mem_count):
+        pl.semaphore_signal(barrier, inc=1, device_id={"mem": (me + d) % mem_count}, device_id_type=MESH)
+    for other in (tx, ty):
+        pl.semaphore_signal(barrier, inc=1, device_id={"tensor": other}, device_id_type=MESH)
+
+    loads = [
+        pltpu.make_async_copy(tokens, tok.at[t], load_sem.at[0]),
+        pltpu.make_async_copy(outgoing.at[me], enc.at[t, me], load_sem.at[1]),
+        pltpu.make_async_copy(w_key, wk, load_sem.at[2]),
+        pltpu.make_async_copy(w_value, wv, load_sem.at[3]),
+        pltpu.make_async_copy(w_out, wo.at[me], load_sem.at[4]),
+    ]
+    wq_loads = []
+    for i, b in enumerate((t, tx, ty, td)):
+        wq_loads.append(pltpu.make_async_copy(w_query.at[b], wq.at[b], load_sem.at[5 + i]))
+    for copy in loads[:2] + wq_loads + loads[2:]:
+        copy.start()
+    pl.semaphore_wait(barrier, mem_count + 1)
+
+    bank_copies = []
+    for d in range(1, mem_count):
+        to = (me + d) % mem_count
+        copy = remote(outgoing.at[to], enc.at[t, me], bank_send.at[d], bank_recv.at[me], mem=to)
+        copy.start()
+        bank_copies.append(copy)
+
+    tok_copies = []
+    for c in range(2):
+        part = pl.ds(c * half, half)
+        for n, other in enumerate((tx, ty)):
+            copy = remote(
+                tokens.at[part], tok.at[t, part], tok_send.at[2 * n + c], tok_recv.at[2 * n + c], tensor=other
+            )
+            copy.start()
+            tok_copies.append(copy)
+
+    @pl.when(z < z_count - 1)
+    def _():
+        remote(w_out, wo.at[me], wo_send.at[0, 0], wo_recv.at[0, 1], mem=me + 2).start()
+
+    @pl.when(z > 0)
+    def _():
+        remote(w_out, wo.at[me], wo_send.at[1, 0], wo_recv.at[1, 1], mem=me - 2).start()
+
+    remote(w_out, wo.at[me], core_send.at[z], core_recv.at[z], mem=mate).start()
+
+    def pass_on(s):
+        @pl.when(z >= s)
+        def _():
+            ref = wo.at[me - 2 * s]
+            arrived(ref, wo_send.at[0, s], wo_recv.at[0, s])
+            remote(ref, ref, core_send.at[z - s], core_recv.at[z - s], mem=mate).start()
+            if s < z_count - 1:
+                @pl.when(z < z_count - 1)
+                def _():
+                    remote(ref, ref, wo_send.at[0, s], wo_recv.at[0, s + 1], mem=me + 2).start()
+
+        @pl.when(z + s < z_count)
+        def _():
+            ref = wo.at[me + 2 * s]
+            arrived(ref, wo_send.at[1, s], wo_recv.at[1, s])
+            remote(ref, ref, core_send.at[z + s], core_recv.at[z + s], mem=mate).start()
+            if s < z_count - 1:
+                @pl.when(z > 0)
+                def _():
+                    remote(ref, ref, wo_send.at[1, s], wo_recv.at[1, s + 1], mem=me - 2).start()
+
+    def add_queries(b, first):
+        @pl.loop(0, width // tile)
+        def _(n):
+            cols = pl.ds(pl.multiple_of(n * tile, tile), tile)
+            term = jnp.dot(tok[b], wq[b, :, cols], preferred_element_type=jnp.float32)
+            if first:
+                acc[:, cols] = term
+            else:
+                acc[:, cols] += term
+
+    enc_rows = enc.shape[1] * enc.shape[2]
+    enc_width = enc.shape[3]
+    slots = keys.shape[1]
+    length = keys.shape[2]
+
+    def make_kv(b):
+        @pl.loop(0, width // tile)
+        def _(n):
+            cols = pl.ds(pl.multiple_of(n * tile, tile), tile)
+            block = enc[b].reshape(enc_rows, enc_width)
+            k = jnp.dot(block, wk[:, cols], preferred_element_type=jnp.float32)
+            keys[b, :, :, cols] = k.astype(jnp.bfloat16).reshape(slots, length, tile)
+            v = jnp.dot(block, wv[:, cols], preferred_element_type=jnp.float32)
+            values[b, :, :, cols] = v.astype(jnp.bfloat16).reshape(slots, length, tile)
+
+    loads[0].wait()
+    wq_loads[0].wait()
+    add_queries(t, True)
+
+    near_copies = []
+    loads[1].wait()
+    order = [0] + [d for k in range(1, mem_count // 2 + 1) for d in sorted({k, mem_count - k})]
+    for d in order:
+        frm = (me + d) % mem_count
+        ref = enc.at[t, frm]
+        if d:
+            arrived(ref, bank_send.at[0], bank_recv.at[frm])
+        for n, other in enumerate((tx, ty)):
+            copy = remote(ref, ref, near_send.at[n, frm], near_recv.at[n, frm], tensor=other)
+            copy.start()
+            near_copies.append(copy)
+
+    for c, b, other in ((0, tx, ty), (1, ty, tx)):
+        ref = tok.at[b, pl.ds(c * half, half)]
+        arrived(ref, tok_send.at[4 + c], tok_recv.at[2 * c + c])
+        copy = remote(ref, ref, tok_send.at[4 + c], tok_recv.at[4 + c], tensor=other)
+        copy.start()
+        tok_copies.append(copy)
+
+    pass_on(1)
+    loads[2].wait()
+    loads[3].wait()
+    make_kv(t)
+    arrived(tok.at[tx, pl.ds(half, half)], tok_send.at[0], tok_recv.at[1])
+    wq_loads[1].wait()
+    add_queries(tx, False)
+    arrived(tok.at[ty, pl.ds(0, half)], tok_send.at[0], tok_recv.at[2])
+    wq_loads[2].wait()
+    add_queries(ty, False)
+
+    for i in range(0, mem_count, 2):
+        for n, b, other in ((0, tx, ty), (1, ty, tx)):
+            ref = enc.at[b, i + n]
+            arrived(ref, near_send.at[2, i + n], near_recv.at[n, i + n])
+            copy = remote(ref, ref, near_send.at[2, i + n], near_recv.at[2, i + n], tensor=other)
+            copy.start()
+            near_copies.append(copy)
+    if z_count > 2:
+        pass_on(2)
+    for i in range(1, mem_count, 2):
+        arrived(enc.at[tx, i], near_send.at[0, 0], near_recv.at[0, i])
+    make_kv(tx)
+    for i in range(0, mem_count, 2):
+        arrived(enc.at[ty, i], near_send.at[0, 0], near_recv.at[1, i])
+    make_kv(ty)
+    arrived(tok.at[td, pl.ds(0, half)], tok_send.at[0], tok_recv.at[4])
+    arrived(tok.at[td, pl.ds(half, half)], tok_send.at[0], tok_recv.at[5])
+    wq_loads[3].wait()
+    add_queries(td, False)
+    queries[...] = (acc[...] * score_scale).astype(jnp.bfloat16)
+    for i in range(mem_count):
+        arrived(enc.at[td, i], near_send.at[0, 0], near_recv.at[2, i])
+    make_kv(td)
+
+    span_rows = rows // spans
+
+    @pl.loop(0, spans)
+    def _(c):
+        first = source[NB * c]
+        second = source[NB * c + 1]
+        where = pl.ds(pl.multiple_of(c * span_rows, span_rows), span_rows)
+        for h in range(width // DH):
+            cols = slice(h * DH, (h + 1) * DH)
+            k = jnp.concatenate(
+                [keys[b, s, :, cols] for s in (first, second) for b in range(tensor_count)], axis=0
+            )
+            v = jnp.concatenate(
+                [values[b, s, :, cols] for s in (first, second) for b in range(tensor_count)], axis=0
+            )
+            scores = lax.dot_general(
+                queries[where, cols], k, (((1,), (1,)), ((), ())), preferred_element_type=jnp.float32
+            )
+            lifted = jnp.exp(scores - jnp.max(scores, axis=-1, keepdims=True))
+            weights = (lifted * (1.0 / jnp.sum(lifted, axis=-1, keepdims=True))).astype(jnp.bfloat16)
+            attended[where, cols] = jnp.dot(weights, v, preferred_element_type=jnp.float32).astype(jnp.bfloat16)
+
+    for s in range(3, z_count):
+        pass_on(s)
+    loads[4].wait()
+    for i in range(z_count):
+        arrived(wo.at[2 * i + 1 - core], core_send.at[0], core_recv.at[i])
+
+    per = mem_count // tensor_count
+    wide = wo.shape[2]
+
+    def project(b, lo, out, extra=None, at=0):
+        @pl.loop(0, per)
+        def _(j):
+            @pl.loop(0, wide // tile)
+            def _(n):
+                inner = pl.ds(pl.multiple_of(n * tile, tile), tile)
+                outer = pl.ds(pl.multiple_of(j * wide + n * tile, tile), tile)
+                term = jnp.dot(
+                    attended[lo : lo + half], wo[b * per + j, :, inner], preferred_element_type=jnp.float32
+                ).astype(jnp.bfloat16)
+                if extra is not None:
+                    term = (term.astype(jnp.float32) + extra[:, outer].astype(jnp.float32)).astype(jnp.bfloat16)
+                out[lo : lo + half, outer] = term
+
+    red_copies = []
+
+    def give(ref, dst, i, other):
+        copy = remote(ref, dst, red_send.at[i], red_recv.at[i], tensor=other)
+        copy.start()
+        red_copies.append(copy)
+
+    low, high = pl.ds(0, half), pl.ds(half, half)
+    project(td, 0, part_d)
+    give(part_d.at[low], relay_x, 0, tx)
+    project(td, half, part_d)
+    give(part_d.at[high], relay_y, 1, ty)
+    project(tx, 0, part_x)
+    give(part_x.at[low], got_x.at[low], 2, tx)
+    project(ty, half, part_y)
+    give(part_y.at[high], got_y.at[high], 3, ty)
+    arrived(relay_x, red_send.at[0], red_recv.at[0])
+    project(ty, 0, part_y, relay_x)
+    give(part_y.at[low], got_y.at[low], 4, ty)
+    arrived(relay_y, red_send.at[0], red_recv.at[1])
+    project(tx, half, part_x, relay_y)
+    give(part_x.at[high], got_x.at[high], 5, tx)
+    red_copies[0].wait_send()
+    red_copies[1].wait_send()
+    project(t, 0, part_d)
+    project(t, half, part_d)
+    for i, ref in ((2, got_x.at[low]), (3, got_y.at[high]), (4, got_y.at[low]), (5, got_x.at[high])):
+        arrived(ref, red_send.at[0], red_recv.at[i])
+    result[...] = (
+        part_d[...].astype(jnp.float32) + got_x[...].astype(jnp.float32) + got_y[...].astype(jnp.float32)
+    ).astype(jnp.bfloat16)
+
+    for copy in bank_copies + tok_copies + near_copies + red_copies[2:]:
+        copy.wait_send()
+    for s in range(z_count - 1):
+        @pl.when((z < z_count - 1) & (z >= s))
+        def _():
+            left(wo.at[0], wo_send.at[0, s], wo_recv.at[0, 0])
+
+        @pl.when((z > 0) & (z + s < z_count))
+        def _():
+            left(wo.at[0], wo_send.at[1, s], wo_recv.at[0, 0])
+    for i in range(z_count):
+        left(wo.at[0], core_send.at[i], core_recv.at[0])
+
+
+def fused_body(tokens, neighbours, memory_bank, w_query, w_key, w_value, w_out):
+    mem_count = lax.axis_size("mem")
+    tensor_count = lax.axis_size("tensor")
+    mem_index = lax.axis_index("mem")
+    slice_len, enc_width = memory_bank.shape[1:]
+    requests = neighbours.shape[0] * neighbours.shape[1] // mem_count
+    spans = requests // NB
+    slot_count = requests // mem_count
+    rows, width = tokens.shape
+    listing = neighbours.reshape(mem_count, requests, 2)
+    owner_ids = listing[:, :, 0]
+    row_ids = listing[:, :, 1]
+    owned_here = owner_ids == mem_index
+    slot_rank = jnp.cumsum(owned_here.astype(jnp.int32), axis=1) - 1
+    slot_ids = jnp.arange(slot_count, dtype=jnp.int32)
+    chosen = owned_here[:, None, :] & (slot_rank[:, None, :] == slot_ids[None, :, None])
+    wanted = jnp.sum(jnp.where(chosen, row_ids[:, None, :], 0), axis=2)
+    outgoing = jnp.take(memory_bank, wanted.reshape(-1), axis=0, mode="clip").reshape(
+        mem_count, slot_count * slice_len, enc_width
+    )
+    own_owner = lax.dynamic_index_in_dim(listing, mem_index, 0, keepdims=False)[:, 0]
+    positions = jnp.arange(requests, dtype=jnp.int32)
+    earlier = positions[None, :] < positions[:, None]
+    same_owner = own_owner[:, None] == own_owner[None, :]
+    own_rank = jnp.sum((same_owner & earlier).astype(jnp.int32), axis=1)
+    source = own_owner * slot_count + own_rank
+    z_count = mem_count // 2
+    bf16 = jnp.bfloat16
+    half = rows // 2
+    slots = mem_count * slot_count
+    hbm = pl.BlockSpec(memory_space=pl.ANY)
+    dma = pltpu.SemaphoreType.DMA
+    return pl.pallas_call(
+        functools.partial(fused_kernel, mem_count, tensor_count, spans, 1.0 / math.sqrt(DH)),
+        out_shape=jax.ShapeDtypeStruct((rows, width), bf16),
+        in_specs=[pl.BlockSpec(memory_space=pltpu.SMEM)] + [hbm] * 6,
+        out_specs=pl.BlockSpec(memory_space=pltpu.VMEM),
+        scratch_shapes=[
+            pltpu.VMEM((tensor_count, rows, width), bf16),
+            pltpu.VMEM((tensor_count, width, width), bf16),
+            pltpu.VMEM((enc_width, width), bf16),
+            pltpu.VMEM((enc_width, width), bf16),
+            pltpu.VMEM((tensor_count, mem_count, slot_count * slice_len, enc_width), bf16),
+            pltpu.VMEM((tensor_count, slots, slice_len, width), bf16),
+            pltpu.VMEM((tensor_count, slots, slice_len, width), bf16),
+            pltpu.VMEM((rows, width), jnp.float32),
+            pltpu.VMEM((rows, width), bf16),
+            pltpu.VMEM((rows, width), bf16),
+            pltpu.VMEM((mem_count,) + w_out.shape, bf16),
+            pltpu.VMEM((rows, width), bf16),
+            pltpu.VMEM((rows, width), bf16),
+            pltpu.VMEM((rows, width), bf16),
+            pltpu.VMEM((half, width), bf16),
+            pltpu.VMEM((half, width), bf16),
+            pltpu.VMEM((rows, width), bf16),
+            pltpu.VMEM((rows, width), bf16),
+            dma((9,)),
+            dma((6,)),
+            dma((6,)),
+            dma((mem_count,)),
+            dma((mem_count,)),
+            dma((3, mem_count)),
+            dma((3, mem_count)),
+            dma((2, z_count)),
+            dma((2, z_count)),
+            dma((z_count,)),
+            dma((z_count,)),
+            dma((6,)),
+            dma((6,)),
+        ],
+        compiler_params=pltpu.CompilerParams(
+            collective_id=0, has_side_effects=True, vmem_limit_bytes=58 * 1024 * 1024
+        ),
+    )(source, tokens, outgoing, w_query.reshape(tensor_count, width, width), w_key, w_value, w_out)
+
+
+def fits(mesh, tokens, neighbours, memory_bank, w_query):
+    mem_count, tensor_count = mesh.shape["mem"], mesh.shape["tensor"]
+    requests = neighbours.shape[0] * neighbours.shape[1] // mem_count
+    return (
+        tensor_count == 4
+        and mem_count % tensor_count == 0
+        and requests == NB * mem_count
+        and tokens.shape[1] == w_query.shape[1]
+    )
+
+
 def solution(mesh):
-    return jax.shard_map(
-        body,
-        mesh=mesh,
-        in_specs=(
-            P("mem", "tensor"),
-            P(),
-            P("mem", "tensor", None),
-            P(None, "tensor"),
-            P(None, "tensor"),
-            P(None, "tensor"),
-            P("tensor", "mem"),
-        ),
-        out_specs=P("mem", "tensor"),
-        check_vma=False,
-    )
+    def run(*args):
+        chosen = fused_body if fits(mesh, *args[:4]) else body
+        return jax.shard_map(
+            chosen,
+            mesh=mesh,
+            in_specs=(
+                P("mem", "tensor"),
+                P(),
+                P("mem", "tensor", None),
+                P(None, "tensor"),
+                P(None, "tensor"),
+                P(None, "tensor"),
+                P("tensor", "mem"),
+            ),
+            out_specs=P("mem", "tensor"),
+            check_vma=False,
+        )(*args)
+
+    return run

time: 266 us -> 156 us (0.59)
  waiting for transfers between devices: 186 us -> 0 us
  Pallas kernels: 0 us -> 148 us
  matrix products: 43.2 us -> 0 us
  between operations: 13.3 us -> 0.04 us
  starting transfers between devices: 6.44 us -> 0 us
  local copies, waits for them, and re-layouts: 13.1 us -> 6.91 us
  other arithmetic: 3.89 us -> 1.11 us
    pallas_call x0 -> x1, Pallas kernels: none -> 148 us  [fused_body(): pl.pallas_call(functools.partial(fused_kernel, mem_count, tensor_count, s...]
    all_gather x3 -> x0, waiting for transfers between devices: 110 us -> none  [the longest x1 49.5 us: body(): lax.all_gather(w_out, 'mem', axis=1, tiled=True)]
    reduce_scatter x1 -> x0, waiting for transfers between devices: 51.4 us -> none  [body(): lax.psum_scatter(partial_value.astype(jnp.bfloat16), 'tensor', scatter_di...]
    dot_general x5 -> x0, matrix products: 43.2 us -> none  [the longest x1 12 us: body(): jnp.einsum('chqk,ckhd->cqhd', weights, value_block, preferred_element_typ...]
    all_to_all x1 -> x0, waiting for transfers between devices: 23.5 us -> none  [body(): lax.all_to_all(outgoing, 'mem', split_axis=0, concat_axis=0, tiled=True)]
    all_to_all x1 -> x0, starting transfers between devices: 6.33 us -> none  [body(): lax.all_to_all(outgoing, 'mem', split_axis=0, concat_axis=0, tiled=True)]
    unnamed x8 -> x2, local copies, waits for them, and re-layouts: 7.16 us -> 3.04 us
  transfers between devices with their start and end apart: 5 -> 0, of which waited for: 5 -> 0; matrix products, arithmetic and copies ran while one was open for 18% -> 0% of each run, Pallas kernels for 0% -> 0%
where the time goes in v1:
time: 156 us
  Pallas kernels  148 us (95%)
  local copies, waits for them, and re-layouts  6.91 us (4%)
    pallas_call x1, Pallas kernels, fused_body(): pl.pallas_call(functools.partial(fused_kernel, mem_count, tensor_count, s...  148 us
    gather x1, local copies, waits for them, and re-layouts, fused_body(): jnp.take(memory_bank, wanted.reshape(-1), axis=0, mode='clip')  3.61 us

profile of v1, /device:TPU:0, one launch (start us, length us, event | category | flops | bytes accessed | tf_op | source)
XLA Modules:
  0.0 156.1 jit_solution(8537512502077424671)
XLA Ops:
  0.0 0.8 copy.10
  0.8 0.1 reshape.32
  0.9 0.2 convert_reduce_fusion
  1.1 0.6 multiply_add_fusion.source
  1.7 0.2 reduce_window_sum.11
  1.9 0.1 select_reduce_fusion
  2.0 0.1 copy.11
  2.1 0.1 reshape.37
  2.2 3.6 %gather_fusion = bf16[16,32,896]{2,1,0:T(8,128)(2,1)} fusion(bf16[64,32,896]{2,1,0:T(8,128)(2,1)} %param.9, s32[1024]{0:T(1024)S(1)} %pad_clamp_fusion), kind=kCustom, calls=%fused_computation | custom fusion | bytes 1835072 | tf_op jit(solution)/shard_map/jit(_take)/gather | solution.py:383
  5.8 148.1 %shard_map.73 = bf16[512,1024]{1,0:T(8,128)(2,1)} custom-call(s32[16]{0:T(128)} %multiply_add_fusion.source, bf16[512,1024]{1,0:T(8,128)(2,1)} %tokens.1, bf16[8,64,896]{2,1,0:T(8,128)(2,1)} %bitcast.15, bf16[4,1024,1024]{2,1,0:T(8,128)(2,1)} %bitcast.14, bf16[896,1024]{1,0:T(8,128)(2,1)} %w_key.1, bf16[896,1024]{1,0:T(8,128)(2,1)} %w_value.1, ...), custom_call_target="tpu_custom_call" | custom-call | tf_op jit(solution)/shard_map/pallas_call | solution.py:398
  153.9 2.3 %copy.13 = bf16[512,1024]{1,0:T(8,128)(2,1)} copy(bf16[512,1024]{1,0:T(8,128)(2,1)} %shard_map.73) | data formatting | bytes 2097152
  (6 shorter events, 0.0 us)

commit v2 on v1

--- a/solution.py
+++ b/solution.py
@@ -274,82 +274,148 @@
 
     span_rows = rows // spans
 
-    @pl.loop(0, spans)
-    def _(c):
-        first = source[NB * c]
-        second = source[NB * c + 1]
-        where = pl.ds(pl.multiple_of(c * span_rows, span_rows), span_rows)
-        for h in range(width // DH):
-            cols = slice(h * DH, (h + 1) * DH)
-            k = jnp.concatenate(
-                [keys[b, s, :, cols] for s in (first, second) for b in range(tensor_count)], axis=0
-            )
-            v = jnp.concatenate(
-                [values[b, s, :, cols] for s in (first, second) for b in range(tensor_count)], axis=0
-            )
-            scores = lax.dot_general(
-                queries[where, cols], k, (((1,), (1,)), ((), ())), preferred_element_type=jnp.float32
-            )
-            lifted = jnp.exp(scores - jnp.max(scores, axis=-1, keepdims=True))
-            weights = (lifted * (1.0 / jnp.sum(lifted, axis=-1, keepdims=True))).astype(jnp.bfloat16)
-            attended[where, cols] = jnp.dot(weights, v, preferred_element_type=jnp.float32).astype(jnp.bfloat16)
-
-    for s in range(3, z_count):
-        pass_on(s)
-    loads[4].wait()
-    for i in range(z_count):
-        arrived(wo.at[2 * i + 1 - core], core_send.at[0], core_recv.at[i])
-
-    per = mem_count // tensor_count
+    def attend(stage):
+        @pl.loop(stage * spans // 2, (stage + 1) * spans // 2)
+        def _(c):
+            first = source[NB * c]
+            second = source[NB * c + 1]
+            where = pl.ds(pl.multiple_of(c * span_rows, span_rows), span_rows)
+            for h in range(width // DH):
+                cols = slice(h * DH, (h + 1) * DH)
+                k = jnp.concatenate(
+                    [keys[b, s, :, cols] for s in (first, second) for b in range(tensor_count)], axis=0
+                )
+                v = jnp.concatenate(
+                    [values[b, s, :, cols] for s in (first, second) for b in range(tensor_count)], axis=0
+                )
+                scores = lax.dot_general(
+                    queries[where, cols], k, (((1,), (1,)), ((), ())), preferred_element_type=jnp.float32
+                )
+                lifted = jnp.exp(scores - jnp.max(scores, axis=-1, keepdims=True))
+                weights = (lifted * (1.0 / jnp.sum(lifted, axis=-1, keepdims=True))).astype(jnp.bfloat16)
+                attended[where, cols] = jnp.dot(weights, v, preferred_element_type=jnp.float32).astype(jnp.bfloat16)
+
     wide = wo.shape[2]
-
-    def project(b, lo, out, extra=None, at=0):
-        @pl.loop(0, per)
+    quarter = half // 2
+
+    def project(b, lo, out, extra=None, count=quarter):
+        @pl.loop(0, 2)
         def _(j):
             @pl.loop(0, wide // tile)
             def _(n):
                 inner = pl.ds(pl.multiple_of(n * tile, tile), tile)
                 outer = pl.ds(pl.multiple_of(j * wide + n * tile, tile), tile)
                 term = jnp.dot(
-                    attended[lo : lo + half], wo[b * per + j, :, inner], preferred_element_type=jnp.float32
+                    attended[lo : lo + count], wo[b * 2 + j, :, inner], preferred_element_type=jnp.float32
                 ).astype(jnp.bfloat16)
                 if extra is not None:
                     term = (term.astype(jnp.float32) + extra[:, outer].astype(jnp.float32)).astype(jnp.bfloat16)
-                out[lo : lo + half, outer] = term
-
-    red_copies = []
-
-    def give(ref, dst, i, other):
-        copy = remote(ref, dst, red_send.at[i], red_recv.at[i], tensor=other)
-        copy.start()
-        red_copies.append(copy)
-
-    low, high = pl.ds(0, half), pl.ds(half, half)
-    project(td, 0, part_d)
-    give(part_d.at[low], relay_x, 0, tx)
-    project(td, half, part_d)
-    give(part_d.at[high], relay_y, 1, ty)
-    project(tx, 0, part_x)
-    give(part_x.at[low], got_x.at[low], 2, tx)
-    project(ty, half, part_y)
-    give(part_y.at[high], got_y.at[high], 3, ty)
-    arrived(relay_x, red_send.at[0], red_recv.at[0])
-    project(ty, 0, part_y, relay_x)
-    give(part_y.at[low], got_y.at[low], 4, ty)
-    arrived(relay_y, red_send.at[0], red_recv.at[1])
-    project(tx, half, part_x, relay_y)
-    give(part_x.at[high], got_x.at[high], 5, tx)
-    red_copies[0].wait_send()
-    red_copies[1].wait_send()
-    project(t, 0, part_d)
-    project(t, half, part_d)
-    for i, ref in ((2, got_x.at[low]), (3, got_y.at[high]), (4, got_y.at[low]), (5, got_x.at[high])):
-        arrived(ref, red_send.at[0], red_recv.at[i])
-    result[...] = (
-        part_d[...].astype(jnp.float32) + got_x[...].astype(jnp.float32) + got_y[...].astype(jnp.float32)
-    ).astype(jnp.bfloat16)
-
-    for copy in bank_copies + tok_copies + near_copies + red_copies[2:]:
+                out[lo : lo + count, outer] = term
+
+    def give(ref, dst, stage, i, other):
+        remote(ref, dst, red_send.at[stage, i], red_recv.at[stage, i], tensor=other).start()
+
+    def need(b, stage):
+        if stage == 0:
+            arrived(wo.at[2 * b + 1 - core], core_send.at[0], core_recv.at[b])
+
+    def far():
+        for s in range(3, z_count):
+            pass_on(s)
+
+    def places(stage):
+        lo = stage * half
+        return lo, lo + quarter, pl.ds(lo, quarter), pl.ds(lo + quarter, quarter), pl.ds(stage * quarter, quarter)
+
+    def plain_x(stage):
+        lo, hi, low, high, relay = places(stage)
+        need(tx, stage)
+        project(tx, lo, part_x)
+        give(part_x.at[low], got_x.at[low], stage, 2, tx)
+
+    def plain_y(stage):
+        lo, hi, low, high, relay = places(stage)
+        need(ty, stage)
+        project(ty, hi, part_y)
+        give(part_y.at[high], got_y.at[high], stage, 3, ty)
+
+    def diagonal(stage):
+        lo, hi, low, high, relay = places(stage)
+        need(td, stage)
+        project(td, lo, part_d)
+        give(part_d.at[low], relay_x.at[relay], stage, 0, tx)
+        project(td, hi, part_d)
+        give(part_d.at[high], relay_y.at[relay], stage, 1, ty)
+
+    def relayed(stage):
+        lo, hi, low, high, relay = places(stage)
+        arrived(relay_x.at[relay], red_send.at[0, 0], red_recv.at[stage, 0])
+        project(ty, lo, part_y, relay_x.at[relay])
+        give(part_y.at[low], got_y.at[low], stage, 4, ty)
+        arrived(relay_y.at[relay], red_send.at[0, 0], red_recv.at[stage, 1])
+        project(tx, hi, part_x, relay_y.at[relay])
+        give(part_x.at[high], got_x.at[high], stage, 5, tx)
+
+    attend(0)
+    loads[4].wait()
+    at_end = (z == 0) | (z == z_count - 1)
+    last = z_count - 1 - z
+    x_late = at_end & (tx == last)
+    y_late = at_end & (ty == last)
+    d_late = at_end & (td == last)
+
+    @pl.when(x_late)
+    def _():
+        plain_y(0)
+        diagonal(0)
+        far()
+        plain_x(0)
+
+    @pl.when(y_late)
+    def _():
+        plain_x(0)
+        diagonal(0)
+        far()
+        plain_y(0)
+
+    @pl.when(d_late)
+    def _():
+        plain_x(0)
+        plain_y(0)
+        far()
+        diagonal(0)
+
+    @pl.when(jnp.logical_not(x_late | y_late | d_late))
+    def _():
+        plain_x(0)
+        plain_y(0)
+        diagonal(0)
+        far()
+
+    attend(1)
+    plain_x(1)
+    plain_y(1)
+    diagonal(1)
+    relayed(0)
+    relayed(1)
+    need(t, 0)
+    for stage in range(2):
+        lo, hi, low, high, relay = places(stage)
+        left(part_d.at[low], red_send.at[stage, 0], red_recv.at[0, 0])
+        left(part_d.at[high], red_send.at[stage, 1], red_recv.at[0, 0])
+    project(t, 0, part_d, count=rows)
+    for stage in range(2):
+        lo, hi, low, high, relay = places(stage)
+        for i, ref in ((2, got_x.at[low]), (3, got_y.at[high]), (4, got_y.at[low]), (5, got_x.at[high])):
+            arrived(ref, red_send.at[0, 0], red_recv.at[stage, i])
+        where = pl.ds(lo, half)
+        result[where] = (
+            part_d[where].astype(jnp.float32) + got_x[where].astype(jnp.float32) + got_y[where].astype(jnp.float32)
+        ).astype(jnp.bfloat16)
+        for i in range(2, 6):
+            left(part_x.at[low], red_send.at[stage, i], red_recv.at[0, 0])
+
+    for copy in bank_copies + tok_copies + near_copies:
         copy.wait_send()
     for s in range(z_count - 1):
         @pl.when((z < z_count - 1) & (z >= s))
@@ -430,8 +496,8 @@
             dma((2, z_count)),
             dma((z_count,)),
             dma((z_count,)),
-            dma((6,)),
-            dma((6,)),
+            dma((2, 6)),
+            dma((2, 6)),
         ],
         compiler_params=pltpu.CompilerParams(
             collective_id=0, has_side_effects=True, vmem_limit_bytes=58 * 1024 * 1024
@@ -444,7 +510,7 @@
     requests = neighbours.shape[0] * neighbours.shape[1] // mem_count
     return (
         tensor_count == 4
-        and mem_count % tensor_count == 0
+        and mem_count == 2 * tensor_count
         and requests == NB * mem_count
         and tokens.shape[1] == w_query.shape[1]
     )

time: 156 us -> 148 us (0.949)
  Pallas kernels: 148 us -> 140 us
    pallas_call x1, Pallas kernels: 148 us -> 140 us  [fused_body(): pl.pallas_call(functools.partial(fused_kernel, mem_count, tensor_count, s...]
where the time goes in v2:
time: 148 us
  Pallas kernels  140 us (95%)
  local copies, waits for them, and re-layouts  6.91 us (5%)
    pallas_call x1, Pallas kernels, fused_body(): pl.pallas_call(functools.partial(fused_kernel, mem_count, tensor_count, s...  140 us
    gather x1, local copies, waits for them, and re-layouts, fused_body(): jnp.take(memory_bank, wanted.reshape(-1), axis=0, mode='clip')  3.61 us
    unnamed x2, local copies, waits for them, and re-layouts  3.04 us

profile of v2, /device:TPU:0, one launch (start us, length us, event | category | flops | bytes accessed | tf_op | source)
XLA Modules:
  0.0 148.3 jit_solution(6322365470845375603)
XLA Ops:
  0.0 0.8 copy.10
  0.8 0.1 reshape.32
  0.9 0.2 convert_reduce_fusion
  1.1 0.6 multiply_add_fusion.source
  1.7 0.2 reduce_window_sum.11
  1.9 0.1 select_reduce_fusion
  2.0 0.1 copy.11
  2.1 0.1 reshape.37
  2.2 3.6 %gather_fusion = bf16[16,32,896]{2,1,0:T(8,128)(2,1)} fusion(bf16[64,32,896]{2,1,0:T(8,128)(2,1)} %param.9, s32[1024]{0:T(1024)S(1)} %pad_clamp_fusion), kind=kCustom, calls=%fused_computation | custom fusion | bytes 1835072 | tf_op jit(solution)/shard_map/jit(_take)/gather | solution.py:449
  5.8 140.2 %shard_map.73 = bf16[512,1024]{1,0:T(8,128)(2,1)} custom-call(s32[16]{0:T(128)} %multiply_add_fusion.source, bf16[512,1024]{1,0:T(8,128)(2,1)} %tokens.1, bf16[8,64,896]{2,1,0:T(8,128)(2,1)} %bitcast.15, bf16[4,1024,1024]{2,1,0:T(8,128)(2,1)} %bitcast.14, bf16[896,1024]{1,0:T(8,128)(2,1)} %w_key.1, bf16[896,1024]{1,0:T(8,128)(2,1)} %w_value.1, ...), custom_call_target="tpu_custom_call" | custom-call | tf_op jit(solution)/shard_map/pallas_call | solution.py:464
  146.0 2.3 %copy.13 = bf16[512,1024]{1,0:T(8,128)(2,1)} copy(bf16[512,1024]{1,0:T(8,128)(2,1)} %shard_map.73) | data formatting | bytes 2097152
  (6 shorter events, 0.0 us)

commit v3 on v2

--- a/solution.py
+++ b/solution.py
@@ -157,16 +157,6 @@
             copy.start()
             tok_copies.append(copy)
 
-    @pl.when(z < z_count - 1)
-    def _():
-        remote(w_out, wo.at[me], wo_send.at[0, 0], wo_recv.at[0, 1], mem=me + 2).start()
-
-    @pl.when(z > 0)
-    def _():
-        remote(w_out, wo.at[me], wo_send.at[1, 0], wo_recv.at[1, 1], mem=me - 2).start()
-
-    remote(w_out, wo.at[me], core_send.at[z], core_recv.at[z], mem=mate).start()
-
     def pass_on(s):
         @pl.when(z >= s)
         def _():
@@ -229,6 +219,16 @@
             copy = remote(ref, ref, near_send.at[n, frm], near_recv.at[n, frm], tensor=other)
             copy.start()
             near_copies.append(copy)
+
+    @pl.when(z < z_count - 1)
+    def _():
+        remote(w_out, wo.at[me], wo_send.at[0, 0], wo_recv.at[0, 1], mem=me + 2).start()
+
+    @pl.when(z > 0)
+    def _():
+        remote(w_out, wo.at[me], wo_send.at[1, 0], wo_recv.at[1, 1], mem=me - 2).start()
+
+    remote(w_out, wo.at[me], core_send.at[z], core_recv.at[z], mem=mate).start()
 
     for c, b, other in ((0, tx, ty), (1, ty, tx)):
         ref = tok.at[b, pl.ds(c * half, half)]

time: 148 us -> 150 us (1.014)
  no operation moved by 1% of the time
where the time goes in v3:
time: 150 us; the launch traced here: 149 us
  Pallas kernels  141 us (94%)
  local copies, waits for them, and re-layouts  6.91 us (5%)
    pallas_call x1, Pallas kernels, fused_body(): pl.pallas_call(functools.partial(fused_kernel, mem_count, tensor_count, s...  141 us
    gather x1, local copies, waits for them, and re-layouts, fused_body(): jnp.take(memory_bank, wanted.reshape(-1), axis=0, mode='clip')  3.61 us
    unnamed x2, local copies, waits for them, and re-layouts  3.04 us

profile of v3, /device:TPU:0, one launch (start us, length us, event | category | flops | bytes accessed | tf_op | source)
XLA Modules:
  0.0 149.5 jit_solution(17556690720245993459)
XLA Ops:
  0.0 0.8 copy.10
  0.8 0.1 reshape.32
  0.9 0.2 convert_reduce_fusion
  1.1 0.6 multiply_add_fusion.source
  1.7 0.2 reduce_window_sum.11
  1.9 0.1 select_reduce_fusion
  2.0 0.1 copy.11
  2.1 0.1 reshape.37
  2.2 3.6 %gather_fusion = bf16[16,32,896]{2,1,0:T(8,128)(2,1)} fusion(bf16[64,32,896]{2,1,0:T(8,128)(2,1)} %param.9, s32[1024]{0:T(1024)S(1)} %pad_clamp_fusion), kind=kCustom, calls=%fused_computation | custom fusion | bytes 1835072 | tf_op jit(solution)/shard_map/jit(_take)/gather | solution.py:449
  5.8 141.4 %shard_map.73 = bf16[512,1024]{1,0:T(8,128)(2,1)} custom-call(s32[16]{0:T(128)} %multiply_add_fusion.source, bf16[512,1024]{1,0:T(8,128)(2,1)} %tokens.1, bf16[8,64,896]{2,1,0:T(8,128)(2,1)} %bitcast.15, bf16[4,1024,1024]{2,1,0:T(8,128)(2,1)} %bitcast.14, bf16[896,1024]{1,0:T(8,128)(2,1)} %w_key.1, bf16[896,1024]{1,0:T(8,128)(2,1)} %w_value.1, ...), custom_call_target="tpu_custom_call" | custom-call | tf_op jit(solution)/shard_map/pallas_call | solution.py:464
  147.2 2.3 %copy.13 = bf16[512,1024]{1,0:T(8,128)(2,1)} copy(bf16[512,1024]{1,0:T(8,128)(2,1)} %shard_map.73) | data formatting | bytes 2097152
  (6 shorter events, 0.0 us)
